TPU v7x, 32 devices: a whole 2x2x4 slice. The times are simulated.
32 devices in a mesh: sub: 4 (over z), cgrp: 8 (over y, x, core).
Axes of the slice: x: 2, y: 2, z: 4, core: 2. Of those that a mesh axis runs over, the one named last changes fastest.
Arguments:
- source: float32 [256, 32768], P('sub', 'cgrp'), may hold values from -7.5 to 7.5
- capacity: float32 [256, 32768], P('sub', 'cgrp'), may hold values from 0.01 to 1
- fd_weights: float32 [256, 32768], P('sub', 'cgrp'), may hold values from 0.02 to 1
- fd_modes: float32 [3, 64, 64], replicated, may hold values from -0.75 to 0.75
- face_modes: float32 [2, 128, 64], replicated, may hold values from -0.75 to 0.75
- coarse_map: int32 [4, 8, 6, 128], P('sub', 'cgrp'), may hold values from 0 to 24575, as said below
- fsai_cols: int32 [192, 8], P(('sub', 'cgrp')), may hold values from 0 to 191
- fsai_blocks: float32 [192, 8, 128, 128], P(('sub', 'cgrp')), may hold values from -0.1875 to 0.1875
Outputs:
- solution: float32 [256, 32768], P('sub', 'cgrp')
- residual: float32 [256, 32768], P('sub', 'cgrp')
Inputs may be any that keep to these rules, and one draw needn't show every extreme that they name: `coarse_map`: entries are numbered by owner: with d = s * 8 + t, face f of subdomain (s, t) takes the entries (6 d + f) * 128 to (6 d + f) * 128 + 127, each once, in an order of its own; except that face 0 of a subdomain with s > 0 takes exactly the entries of face 1 of subdomain (s - 1, t), and face 2 of a subdomain with t > 0 exactly those of face 3 of subdomain (s, t - 1), function k of both sides taking the same entry.
All inputs are finite; a program needn't handle non-finite values.
Results may differ from a plain program's by a relative error of at most 0.0001.
Values sent between devices are 32-bit elements; how exact they have to be, the bound alone decides.
A program may use at most 64 MiB of HBM per device.

v0:
```python
import jax
import jax.numpy as jnp
from jax import lax
from jax.sharding import PartitionSpec as P

C = 64


highest = lax.Precision.HIGHEST
along_first = 1.0
along_second = 0.6
along_third = 2.5


def with_halo(array, sides, width):
    for axis, dim in sides:
        count, length = (lax.axis_size(axis), array.shape[dim])
        up = [(i, (i + 1) % count) for i in range(count - 1)]
        down = [(j, i) for i, j in up]
        last = lax.slice_in_dim(array, length - width, length, axis=dim)
        first = lax.slice_in_dim(array, 0, width, axis=dim)
        before = lax.ppermute(last, axis, up)
        after = lax.ppermute(first, axis, down)
        array = jnp.concatenate([before, array, after], axis=dim)
    return array


def operate(field, capacity):
    padded = with_halo(field, (("sub", 0), ("cgrp", 1)), 1)
    padded = jnp.pad(padded, ((0, 0), (0, 0), (1, 1)))
    first = padded[2:, 1:-1, 1:-1] + padded[:-2, 1:-1, 1:-1]
    second = padded[1:-1, 2:, 1:-1] + padded[1:-1, :-2, 1:-1]
    third = padded[1:-1, 1:-1, 2:] + padded[1:-1, 1:-1, :-2]
    diagonal = capacity + 2.0 * (along_first + along_second + along_third)
    return diagonal * field - along_first * first - along_second * second - along_third * third


def transform(blocks, modes):
    blocks = jnp.einsum("ai,...ijk->...ajk", modes[0], blocks, precision=highest)
    blocks = jnp.einsum("bj,...ajk->...abk", modes[1], blocks, precision=highest)
    return jnp.einsum("ck,...abk->...abc", modes[2], blocks, precision=highest)


def transform_back(blocks, modes):
    blocks = jnp.einsum("ai,...ajk->...ijk", modes[0], blocks, precision=highest)
    blocks = jnp.einsum("bj,...ibk->...ijk", modes[1], blocks, precision=highest)
    return jnp.einsum("ck,...ijc->...ijk", modes[2], blocks, precision=highest)


def face_planes(blocks):
    return jnp.stack(
        [
            blocks[..., 0, :, :],
            blocks[..., -1, :, :],
            blocks[..., :, 0, :],
            blocks[..., :, -1, :],
            blocks[..., :, :, 0],
            blocks[..., :, :, -1],
        ],
        axis=-3,
    )


def restrict(planes, face_modes):
    partial_rows = jnp.einsum("ka,...fab->...fkb", face_modes[0], planes, precision=highest)
    return jnp.sum(partial_rows * face_modes[1], axis=-1)


def extend(values, face_modes):
    return jnp.einsum(
        "ka,...fkb->...fab", face_modes[0], values[..., None] * face_modes[1], precision=highest
    )


def add_planes(blocks, planes):
    blocks = blocks.at[..., 0, :, :].add(planes[..., 0, :, :])
    blocks = blocks.at[..., -1, :, :].add(planes[..., 1, :, :])
    blocks = blocks.at[..., :, 0, :].add(planes[..., 2, :, :])
    blocks = blocks.at[..., :, -1, :].add(planes[..., 3, :, :])
    blocks = blocks.at[..., :, :, 0].add(planes[..., 4, :, :])
    blocks = blocks.at[..., :, :, -1].add(planes[..., 5, :, :])
    return blocks


def coarse_apply(coarse, fsai_cols, fsai_blocks):
    table = coarse.reshape(-1, fsai_blocks.shape[2])
    picked = table[fsai_cols]
    image = jnp.einsum("rnij,rnj->ri", fsai_blocks, picked, precision=highest)
    spread = jnp.einsum("rnij,ri->rnj", fsai_blocks, image, precision=highest)
    return jnp.zeros_like(table).at[fsai_cols].add(spread).reshape(-1)


def coarse_round(coarse_local, coarse_map, fsai_cols, fsai_blocks):
    slots = coarse_map.reshape(-1)
    length = fsai_blocks.shape[0] * fsai_blocks.shape[2] * lax.axis_size(("sub", "cgrp"))
    term = jnp.zeros((length,), jnp.float32).at[slots].add(coarse_local.reshape(-1))
    coarse = lax.psum(term, ("sub", "cgrp"))
    back = lax.psum(coarse_apply(coarse, fsai_cols, fsai_blocks), ("sub", "cgrp"))
    return back[slots].reshape(coarse_local.shape)


def precondition(residual, fd_weights, fd_modes, face_modes, coarse_map, fsai_cols, fsai_blocks):
    local = transform_back(fd_weights * transform(residual, fd_modes), fd_modes)
    coarse_local = restrict(face_planes(residual), face_modes)
    correction = coarse_round(coarse_local, coarse_map, fsai_cols, fsai_blocks)
    return add_planes(local, extend(correction, face_modes))


def inner_sum(left, right):
    return lax.psum(jnp.sum(left * right), ("sub", "cgrp"))


def curvature_sum(left, right):
    return lax.psum(jnp.sum(left * right), ("sub", "cgrp"))


def body(source, capacity, fd_weights, fd_modes, face_modes, coarse_map, fsai_cols, fsai_blocks):
    cube = (C, C, C)
    flat_shape = source.shape
    source = source.reshape(cube)
    capacity = capacity.reshape(cube)
    fd_weights = fd_weights.reshape(cube)
    residual = source
    precond = precondition(
        residual, fd_weights, fd_modes, face_modes, coarse_map, fsai_cols, fsai_blocks
    )
    gamma = inner_sum(residual, precond)
    image = operate(precond, capacity)
    alpha = gamma / curvature_sum(precond, image)
    solution = alpha * precond
    residual = residual - alpha * image
    return (solution.reshape(flat_shape), residual.reshape(flat_shape))


def solution(mesh):
    in_specs = (
        P("sub", "cgrp"),
        P("sub", "cgrp"),
        P("sub", "cgrp"),
        P(),
        P(),
        P("sub", "cgrp", None, None),
        P(("sub", "cgrp"), None),
        P(("sub", "cgrp"), None, None, None),
    )
    out_specs = (P("sub", "cgrp"), P("sub", "cgrp"))
    return jax.shard_map(body, mesh=mesh, in_specs=in_specs, out_specs=out_specs, check_vma=False)
```

profile of v0, /device:TPU:0, one launch (start us, length us, event | category | flops | bytes accessed | tf_op | source)
XLA Modules:
  0.0 432.9 jit_solution(17539706606090331872)
XLA Ops:
  13.2 5.0 %fusion.59 = (f32[64,64,1]{2,1,0:T(8,128)}, f32[64,64,1]{2,1,0:T(8,128)}) fusion(f32[64,64,64]{2,1,0:T(8,128)} %reshape.238), kind=kLoop, calls=%fused_computation.103 | loop fusion | bytes 65536 | tf_op jit(solution)/shard_map/slice | solution.py:58
  21.4 3.3 copy.124
  24.6 3.2 copy.123
  32.0 6.5 %scatter_custom_fusion = f32[24576]{0:T(1024)} fusion(s32[768]{0:T(1024)S(1)} %fusion.53, f32[768]{0:T(1024)S(1)} %bitcast.105, f32[]{:T(128)} %constant.167.clone.1), kind=kCustom, calls=%fused_computation.52 | custom fusion | flops 768 | bytes 98308 | tf_op jit(solution)/shard_map/scatter-add | solution.py:96
  38.9 4.6 %fusion.16 = f32[64,64,64]{2,0,1:T(8,128)S(1)} fusion(f32[64,64,64]{2,1,0:T(8,128)} %reshape.238, f32[3,64,64]{2,1,0:T(8,128)S(1)} %copy-done.7), kind=kOutput, calls=%fused_computation.36 | convolution fusion | flops 201326592 | bytes 2129920 | tf_op jit(solution)/shard_map/ai,...ijk->...ajk/dot_general | solution.py:39
  43.5 5.6 %fusion.14 = f32[64,64,64]{2,1,0:T(8,128)} fusion(f32[64,64,64]{2,0,1:T(8,128)S(1)} %fusion.16, f32[3,64,64]{2,1,0:T(8,128)S(1)} %copy-done.7), kind=kOutput, calls=%fused_computation.34 | convolution fusion | flops 201326592 | bytes 3178496 | tf_op jit(solution)/shard_map/bj,...ajk->...abk/dot_general | solution.py:40
  49.1 3.6 reshape.239
  52.7 5.8 %fusion.21 = f32[64,64,64]{2,1,0:T(8,128)S(1)} fusion(f32[64,64,64]{2,1,0:T(8,128)} %reshape.239, f32[64,64,64]{2,1,0:T(8,128)} %fusion.14, f32[3,64,64]{2,1,0:T(8,128)S(1)} %copy-done.7), kind=kOutput, calls=%fused_computation.42 | convolution fusion | flops 201588736 | bytes 3178496 | tf_op jit(solution)/shard_map/ck,...abk->...abc/dot_general | solution.py:41
  58.5 5.6 %fusion.18 = f32[64,64,64]{0,2,1:T(8,128)} fusion(f32[64,64,64]{2,1,0:T(8,128)S(1)} %fusion.21, f32[3,64,64]{2,1,0:T(8,128)S(1)} %copy-done.7), kind=kOutput, calls=%fused_computation.41 | convolution fusion | flops 201326592 | bytes 3178496 | tf_op jit(solution)/shard_map/ai,...ajk->...ijk/dot_general | solution.py:45
  64.1 4.3 copy.80
  68.4 3.5 fusion.40
  71.9 3.4 fusion.8
  75.3 86.6 %all-reduce.5.cloned.1.call-done = f32[192,128]{1,0:T(8,128)} async-done(((f32[192,128]{1,0:T(8,128)}), f32[192,128]{1,0:T(8,128)}) %all-reduce.5.cloned.1.call-update) | async-done | bytes 98320 | tf_op jit(solution)/shard_map/psum | solution.py:97
  169.1 121.4 %all-reduce.7.cloned.1.call-done = f32[24576]{0:T(1024)} async-done(((f32[24576]{0:T(1024)}), f32[24576]{0:T(1024)}) %all-reduce.7.cloned.1.call-update) | async-done | bytes 98320 | tf_op jit(solution)/shard_map/psum | solution.py:98
  290.6 4.8 %gather_fusion.1 = f32[768]{0:T(1024)S(1)} fusion(f32[24576]{0:T(1024)} %all-reduce.7.cloned.1.call-done, s32[1024]{0:T(1024)S(1)} %pad_clamp_fusion), kind=kCustom, calls=%fused_computation.1 | custom fusion | bytes 9216 | tf_op jit(solution)/shard_map/gather | solution.py:99
  299.2 5.1 %scatter-add.48 = f32[64,64,64]{1,2,0:T(8,128)S(1)} dynamic-update-slice(f32[64,64,64]{1,2,0:T(8,128)S(1)} %constant_dynamic-update-slice_fusion.2, f32[64,1,64]{1,2,0:T(8,128)} %copy.95, s32[]{:T(128)} %constant.168.clone.1, s32[]{:T(128)} %constant.168.clone.1, s32[]{:T(128)} %constant.168.clone.1) | dynamic-update-slice | bytes 32772 | tf_op jit(solution)/shard_map/scatter-add | solution.py:78
  310.5 8.4 %scatter-add.49 = f32[64,64,64]{1,2,0:T(8,128)S(1)} dynamic-update-slice(f32[64,64,64]{1,2,0:T(8,128)S(1)} %scatter-add.48, f32[64,1,64]{1,2,0:T(8,128)} %copy.97, s32[]{:T(128)} %constant.168.clone.1, s32[]{:T(128)} %constant.171.clone.1, s32[]{:T(128)} %constant.168.clone.1) | dynamic-update-slice | bytes 32772 | tf_op jit(solution)/shard_map/scatter-add | solution.py:79
  319.4 5.1 %collective-permute-start.1 = (f32[1,64,64]{1,2,0:T(8,128)S(1)}, f32[1,64,64]{1,2,0:T(8,128)S(1)}, u32[]{:S(2)}, u32[]{:S(2)}) collective-permute-start(f32[1,64,64]{1,2,0:T(8,128)S(1)} %get-tuple-element.83), channel_id=1, source_target_pairs={{0,8},{8,16},{16,24},{1,9},{9,17},{17,25},{2,10},{10,18},{18,26},{... | collective-permute-start | bytes 49160 | tf_op jit(solution)/shard_map/ppermute | solution.py:22
  326.1 4.2 collective-permute-done
  344.5 3.2 copy.100
  358.9 3.7 select_maximum_fusion
  363.7 6.5 %multiply_reduce_fusion = (f32[]{:T(128)}, f32[]{:T(128)}, f32[64,64,64]{1,2,0:T(8,128)}) fusion(f32[64,64,64]{1,2,0:T(8,128)S(1)} %scatter-add.51, f32[64,64,64]{1,2,0:T(8,128)S(1)} %copy-done.5, f32[66,66,66]{1,2,0:T(8,128)S(1)} %select_maximum_fusion, f32[1,64,64]{1,2,0:T(8,128)S(1)} %collective-permute-done, f32[1,64,64]{1,2,0:T(8,128)S(1)} %collective-permute-done.1, ...), kind=kLoop, calls=%fused_computation.39 | loop fusion | flops 5505022 | bytes 6358024 | tf_op jit(solution)/shard_map/reduce_sum | solution.py:114
  370.2 39.3 %all-reduce.1 = (f32[]{:T(128)}, f32[]{:T(128)}) all-reduce(f32[]{:T(128)} %get-tuple-element.75, f32[]{:T(128)} %get-tuple-element.74), channel_id=1, replica_groups=mesh['sub'=4,'cgrp'=8] {'sub','cgrp'}, use_global_device_ids=true, to_apply=%region_6.0 | all-reduce | flops 2 | bytes 16 | tf_op jit(solution)/shard_map/psum | solution.py:110
  410.9 5.4 %multiply_subtract_fusion = (f32[64,64,64]{1,2,0:T(8,128)}, f32[64,64,64]{1,2,0:T(8,128)}) fusion(f32[64,64,64]{1,2,0:T(8,128)} %copy.100, f32[64,64,64]{1,2,0:T(8,128)} %get-tuple-element.80, f32[]{:T(128)S(6)} %div.3, f32[64,64,64]{1,2,0:T(8,128)S(1)} %scatter-add.51), kind=kLoop, calls=%fused_computation.38 | loop fusion | flops 786432 | bytes 5242884 | tf_op jit(solution)/shard_map/sub | solution.py:131
  (97 shorter events, 68.8 us)
Async XLA Ops:
  7.2 156.2 %copy-start = (f32[6,8,128,128]{3,2,1,0:T(8,128)S(1)}, f32[6,8,128,128]{3,2,1,0:T(8,128)}, u32[]{:S(2)}) copy-start(f32[6,8,128,128]{3,2,1,0:T(8,128)} %param.27) | copy-start | bytes 9437188
  7.2 154.7 %all-reduce.5.cloned.1.call-start = ((), (), s32[]{:S(2)}) async-start(), calls=%async_computation | async-start | bytes 196608 | tf_op jit(solution)/shard_map/psum | solution.py:97
  13.2 5.0 %copy-start.10 = (s32[1,1,6,128]{3,1,2,0:T(1,128)S(1)}, s32[1,1,6,128]{3,1,2,0:T(1,128)}, u32[]{:S(2)}) copy-start(s32[1,1,6,128]{3,1,2,0:T(1,128)} %param.25) | copy-start | bytes 9220
  13.2 5.0 %copy-start.8 = (f32[2,128,64]{1,2,0:T(8,128)S(1)}, f32[2,128,64]{1,2,0:T(8,128)}, u32[]{:S(2)}) copy-start(f32[2,128,64]{1,2,0:T(8,128)} %param.24) | copy-start | bytes 196612
  21.3 17.5 %copy-start.9 = (s32[6,8]{1,0:T(8,128)S(1)}, s32[6,8]{1,0:T(8,128)}, u32[]{:S(2)}) copy-start(s32[6,8]{1,0:T(8,128)} %param.26) | copy-start | bytes 580
  21.3 17.6 %copy-start.7 = (f32[3,64,64]{2,1,0:T(8,128)S(1)}, f32[3,64,64]{2,1,0:T(8,128)}, u32[]{:S(2)}) copy-start(f32[3,64,64]{2,1,0:T(8,128)} %param.23) | copy-start | bytes 147460
  38.5 252.1 %all-reduce.7.cloned.1.call-start = ((), (), s32[]{:S(2)}) async-start(), calls=%async_computation.1 | async-start | bytes 196608 | tf_op jit(solution)/shard_map/psum | solution.py:98
  166.0 3.0 slice-start
  169.1 127.1 %copy-start.2 = (f32[64,64,64]{1,2,0:T(8,128)S(1)}, f32[64,64,64]{1,2,0:T(8,128)}, u32[]{:S(2)}) copy-start(f32[64,64,64]{1,2,0:T(8,128)} %fusion.8) | copy-start | bytes 3145732
  319.4 6.7 %collective-permute-start.1 = (f32[1,64,64]{1,2,0:T(8,128)S(1)}, f32[1,64,64]{1,2,0:T(8,128)S(1)}, u32[]{:S(2)}, u32[]{:S(2)}) collective-permute-start(f32[1,64,64]{1,2,0:T(8,128)S(1)} %get-tuple-element.83), channel_id=1, source_target_pairs={{0,8},{8,16},{16,24},{1,9},{9,17},{17,25},{2,10},{10,18},{18,26},{... | collective-permute-start | bytes 49160 | tf_op jit(solution)/shard_map/ppermute | solution.py:22
  324.5 5.8 %collective-permute-start = (f32[1,64,64]{1,2,0:T(8,128)S(1)}, f32[1,64,64]{1,2,0:T(8,128)S(1)}, u32[]{:S(2)}, u32[]{:S(2)}) collective-permute-start(f32[1,64,64]{1,2,0:T(8,128)S(1)} %get-tuple-element.84), channel_id=1, source_target_pairs={{8,0},{16,8},{24,16},{9,1},{17,9},{25,17},{10,2},{18,10},{26,18},{... | collective-permute-start | bytes 49160 | tf_op jit(solution)/shard_map/ppermute | solution.py:23
  338.9 17.0 %collective-permute-start.2 = (f32[66,1,64]{0,2,1:T(8,128)S(1)}, f32[66,1,64]{0,2,1:T(8,128)S(1)}, u32[]{:S(2)}, u32[]{:S(2)}) collective-permute-start(f32[66,1,64]{0,2,1:T(8,128)S(1)} %copy.102), channel_id=1, source_target_pairs={{1,0},{2,1},{3,2},{4,3},{5,4},{6,5},{7,6},{9,8},{10,9},{11,10},{12... | collective-permute-start | bytes 50696 | tf_op jit(solution)/shard_map/ppermute | solution.py:23
  340.1 12.7 %collective-permute-start.3 = (f32[66,1,64]{0,2,1:T(8,128)S(1)}, f32[66,1,64]{0,2,1:T(8,128)S(1)}, u32[]{:S(2)}, u32[]{:S(2)}) collective-permute-start(f32[66,1,64]{0,2,1:T(8,128)S(1)} %copy.104), channel_id=1, source_target_pairs={{0,1},{1,2},{2,3},{3,4},{4,5},{5,6},{6,7},{8,9},{9,10},{10,11},{11... | collective-permute-start | bytes 50696 | tf_op jit(solution)/shard_map/ppermute | solution.py:22
  358.9 3.8 copy-start.3
  358.9 3.8 copy-start.4
  358.9 4.2 copy-start.5
  358.9 4.8 %copy-start.6 = (f32[64,64,64]{1,2,0:T(8,128)S(1)}, f32[64,64,64]{1,2,0:T(8,128)}, u32[]{:S(2)}) copy-start(f32[64,64,64]{1,2,0:T(8,128)} %copy.101) | copy-start | bytes 3145732
  419.8 6.0 %copy-start.1 = (f32[6,8,128,128]{3,2,1,0:T(8,128)S(1)}, f32[6,8,128,128]{3,2,1,0:T(8,128)}, u32[]{:S(2)}) copy-start(f32[6,8,128,128]{3,2,1,0:T(8,128)} %param.27) | copy-start | bytes 9437188
Sparse Core Ops, SparseCore 0:
  38.6 123.2 all-reduce.4
  169.1 121.3 all-reduce.6
where the time goes:
time: 439 us; the launch traced here: 433 us
  waiting for transfers between devices  213 us (49%)
  local copies, waits for them, and re-layouts  95.1 us (22%)
  blocking collectives  39.3 us (9%)
  matrix products  33.6 us (8%)
  other arithmetic  25.1 us (6%)
  between operations  16 us (4%)
  starting transfers between devices  11.1 us (3%)
    psum x1, waiting for transfers between devices, coarse_round(): lax.psum(coarse_apply(coarse, fsai_cols, fsai_blocks), ('sub', 'cgrp'))  121 us
    psum x1, waiting for transfers between devices, coarse_round(): coarse = lax.psum(term, ('sub', 'cgrp'))  86.6 us
    psum x1, blocking collectives, inner_sum(): return lax.psum(jnp.sum(left * right), ('sub', 'cgrp'))  39.3 us
    unnamed x35, local copies, waits for them, and re-layouts  15.9 us
  transfers between devices with their start and end apart: 6, of which 4 were waited for; matrix products, arithmetic and copies ran while one was open for 11% of the time, Pallas kernels for 0%

commit v1 on v0

v1 whole, which is shorter than its diff:
```python
import functools
import jax
import jax.numpy as jnp
from jax import lax
from jax.experimental import pallas as pl
from jax.experimental.pallas import tpu as pltpu
from jax.sharding import PartitionSpec as P

C = 64
T = 32
CH = 8
f32 = jnp.float32
bf16 = jnp.bfloat16
HI = lax.Precision.HIGHEST
MESH = pl.DeviceIdType.MESH


def nn(a, b):
    return lax.dot_general(a, b, (((1,), (0,)), ((), ())), precision=HI, preferred_element_type=f32)


def nt(a, b):
    return lax.dot_general(a, b, (((1,), (1,)), ((), ())), precision=HI, preferred_element_type=f32)


def mm(a, b):
    return lax.dot_general(a, b, (((1,), (0,)), ((), ())), preferred_element_type=f32)


def mmt(a, b):
    return lax.dot_general(a, b, (((1,), (1,)), ((), ())), preferred_element_type=f32)


def split(x):
    hi = x.astype(bf16)
    return hi, (x - hi.astype(f32)).astype(bf16)


def iota(shape, dim):
    return lax.broadcasted_iota(jnp.int32, shape, dim)


def left3(m):
    hi, lo = split(m)
    return jnp.concatenate([hi, lo, hi], axis=1)


def rows3(x):
    hi, lo = split(x)
    return jnp.concatenate([hi, hi, lo], axis=0)


def lanes_weights(k):
    hi, lo = split(k)
    top = jnp.concatenate([hi, lo], axis=1)
    bottom = jnp.concatenate([hi, jnp.zeros_like(lo)], axis=1)
    return jnp.concatenate([top, bottom], axis=0)


def lane_transform(x, w):
    hi, lo = split(x)
    r = mm(jnp.concatenate([hi, lo], axis=1), w)
    return r[:, :128] + r[:, 128:]


def kernel(nsub, ncg, x_ref, modes_ref, face_ref, map_ref, cols_ref, cap_any, wt_any, blk_any,
           p_out, img_out, alpha_out,
           s_ref, z_ref, w_ref, p_ref, cap_ref, blk_ref, sel_ref, am_ref, kw_ref,
           ag_ref, send1_ref, a2s_ref, a2r_ref, pick_ref, spread_ref,
           hi_ref, his_ref, hj_ref, hjs_ref, cs_ref, cr_ref,
           dsem, ag_s, ag_r, a2_s, a2_r, h_s, h_r, c_s, c_r):
    n = nsub * ncg
    s = lax.axis_index("sub")
    t = lax.axis_index("cgrp")
    me = s * ncg + t

    def peer(o):
        d = lax.rem(me + o, n)
        return d, (lax.div(d, ncg), lax.rem(d, ncg))

    barrier = pltpu.get_barrier_semaphore()

    @pl.loop(1, n)
    def _(o):
        _, dev = peer(o)
        pl.semaphore_signal(barrier, inc=1, device_id=dev, device_id_type=MESH)

    wcopy = pltpu.make_async_copy(wt_any, w_ref, dsem.at[0])
    bcopy = pltpu.make_async_copy(blk_any, blk_ref, dsem.at[1])
    ccopy = pltpu.make_async_copy(cap_any, cap_ref, dsem.at[2])
    wcopy.start()
    bcopy.start()
    ccopy.start()

    lane = iota((1, 128), 1)
    low = lane < 64
    low32 = jnp.broadcast_to(low, (32, 128))
    low64 = jnp.broadcast_to(low, (64, 128))

    def swap(a):
        return pltpu.roll(a, 64, 1)

    @pl.loop(0, 8)
    def _(c):
        r = iota((128, 512), 0)
        col = iota((128, 512), 1) + c * 512
        hit = ((col >> 6) == (r & 63)) & ((col & 63) == 63 * (r >> 6))
        sel_ref[:, pl.ds(pl.multiple_of(c * 512, 512), 512)] = jnp.where(hit, 1.0, 0.0).astype(bf16)

    for q in range(T):
        s_ref[q * 64 : q * 64 + 64, :] = x_ref[:, q * 128 : q * 128 + 128]

    fm0 = face_ref[0]
    fm1 = face_ref[1]
    r64 = iota((64, 64), 0)
    c64 = iota((64, 64), 1)
    eye64 = jnp.where(r64 == c64, 1.0, 0.0)
    qm = jnp.where(c64 == 2 * (r64 & 31) + (r64 >> 5), 1.0, 0.0)
    dup = jnp.where((iota((64, 128), 1) & 63) == iota((64, 128), 0), 1.0, 0.0)
    dupt = jnp.where((iota((128, 64), 0) & 63) == iota((128, 64), 1), 1.0, 0.0)
    eye128 = jnp.where(iota((128, 128), 0) == iota((128, 128), 1), 1.0, 0.0)
    fm11 = nn(fm1, dup)
    fm0p = nt(fm0, qm)

    y0 = s_ref[pl.ds(0, 32, stride=64), :]
    y1 = s_ref[pl.ds(63, 32, stride=64), :]
    f01 = jnp.concatenate([jnp.where(low32, y0, swap(y1)), jnp.where(low32, swap(y0), y1)], axis=0)
    f23 = jnp.where(low64, s_ref[0:64, :], s_ref[31 * 64 : 32 * 64, :])
    xh, xl = split(x_ref[...])
    f45 = mmt(jnp.concatenate([xh, xl], axis=0), sel_ref[...])
    f45 = f45[:64] + f45[64:]

    mapf = (map_ref[0, 0] & 127).astype(f32)
    mapf = jnp.concatenate([mapf, jnp.zeros((2, 128), f32)], axis=0)
    mapt = nt(eye128, mapf)
    lanef = iota((128, 128), 1).astype(f32)
    rows = []
    for pair, (left, plane) in enumerate(((fm0p, f01), (fm0, f23), (fm0, f45))):
        u = nn(left, plane) * fm11
        for half in range(2):
            keep = low if half == 0 else jnp.logical_not(low)
            val = jnp.sum(jnp.where(keep, u, 0.0), axis=1, keepdims=True)
            f = 2 * pair + half
            place = mapt[:, f : f + 1] == lanef
            rows.append(jnp.sum(jnp.where(place, val, 0.0), axis=0, keepdims=True))
    mine = jnp.concatenate(rows + [jnp.zeros((2, 128), f32)], axis=0)
    send1_ref[...] = mine
    ag_ref[me] = mine

    pl.semaphore_wait(barrier, n - 1)

    @pl.loop(1, n)
    def _(o):
        _, dev = peer(o)
        pltpu.make_async_remote_copy(src_ref=send1_ref, dst_ref=ag_ref.at[me], send_sem=ag_s, recv_sem=ag_r,
                                     device_id=dev, device_id_type=MESH).start()

    m0, m1, m2 = modes_ref[0], modes_ref[1], modes_ref[2]
    am_ref[0] = left3(m0)
    am_ref[1] = left3(nt(eye64, m0))
    am_ref[2] = left3(nt(nn(qm, m1), qm))
    am_ref[3] = left3(nt(nt(qm, m1), qm))
    block = (iota((128, 128), 0) >> 6) == (iota((128, 128), 1) >> 6)
    kw_ref[0] = lanes_weights(jnp.where(block, nn(nt(dupt, m2), dup), 0.0))
    kw_ref[1] = lanes_weights(jnp.where(block, nn(dupt, nn(m2, dup)), 0.0))

    @pl.loop(0, T // CH)
    def _(c):
        base = pl.multiple_of(c * (CH * 128), CH * 128)
        y = mm(am_ref[0], rows3(x_ref[:, pl.ds(base, CH * 128)]))
        stacked = jnp.concatenate([y[:, g * 128 : g * 128 + 128] for g in range(CH)], axis=0)
        s_ref[pl.ds(pl.multiple_of(c * (CH * 64), CH * 64), CH * 64), :] = lane_transform(stacked, kw_ref[0])

    wcopy.wait()
    for q in range(T):
        z_ref[q * 64 : q * 64 + 64, :] = w_ref[:, q * 128 : q * 128 + 128]

    def turned(ref, u):
        a = ref[pl.ds(u, 32, stride=64), :]
        b = ref[pl.ds(u + 32, 32, stride=64), :]
        return jnp.concatenate([jnp.where(low32, a, swap(b)), jnp.where(low32, swap(a), b)], axis=0)

    def middle(c, acc):
        fwd = jnp.concatenate([turned(s_ref, c * CH + g) for g in range(CH)], axis=1)
        wts = jnp.concatenate([turned(z_ref, c * CH + g) for g in range(CH)], axis=1)
        v = mm(am_ref[2], rows3(fwd))
        wv = wts * v
        prod = wv * v
        for g in range(CH):
            acc = acc + prod[:, g * 128 : g * 128 + 128]
        y = mm(am_ref[3], rows3(wv))
        for g in range(CH):
            p_ref[pl.ds(pl.multiple_of(64 + (c * CH + g) * 64, 64), 64), :] = y[:, g * 128 : g * 128 + 128]
        return acc

    gacc = lax.fori_loop(0, T // CH, middle, jnp.zeros((64, 128), f32))

    cols = cols_ref[...]
    nrow = cols.shape[0]
    nz = cols.shape[1]
    wide_cols = jnp.concatenate([jnp.broadcast_to(cols[i : i + 1, :], (nz, nz)) for i in range(nrow)], axis=0)
    kk = nrow * nz
    pick_diag = iota((kk, nz), 1) == (iota((kk, nz), 0) & (nz - 1))
    colv = jnp.sum(jnp.where(pick_diag, wide_cols.astype(f32), 0.0), axis=1, keepdims=True)
    r = iota((1, n * 8), 1)
    d = r >> 3
    f = r & 7
    own = nrow * d + f
    own = jnp.where((f == 0) & (d >= ncg), nrow * (d - ncg) + 1, own)
    own = jnp.where((f == 2) & (lax.rem(d, ncg) > 0), nrow * (d - 1) + 3, own)
    own = jnp.where(f >= 6, -1, own).astype(f32)
    g1 = jnp.where(colv == own, 1.0, 0.0)
    g1 = jnp.concatenate([g1, jnp.zeros((128 - kk, n * 8), f32)], axis=0)

    pltpu.make_async_copy(ag_ref.at[pl.ds(0, n - 1)], ag_ref.at[pl.ds(0, n - 1)], ag_r).wait()
    picked = nn(g1, ag_ref[...].reshape(n * 8, 128))
    pick_ref[...] = picked[:kk].reshape(nrow, nz, 128)
    bcopy.wait()
    spread_ref[...] = jnp.zeros_like(spread_ref)

    def coarse_row(i, acc):
        pk = pick_ref[i]
        tot = blk_ref[i, 0] * pk[0:1]
        for k in range(1, nz):
            tot = tot + blk_ref[i, k] * pk[k : k + 1]
        img = jnp.sum(tot, axis=1, keepdims=True)
        out = [jnp.sum(blk_ref[i, k] * img, axis=0, keepdims=True) for k in range(nz)]
        spread_ref[i] = jnp.concatenate(out, axis=0)
        return acc + img * img

    iacc = lax.fori_loop(0, nrow, coarse_row, jnp.zeros((128, 1), f32))
    gpart = jnp.sum(iacc, keepdims=True) + jnp.sum(gacc, keepdims=True)
    back = nn(g1.T, spread_ref[...].reshape(128, 128))
    back = jnp.where((iota((n * 8, 128), 0) & 7) == 6, gpart, back)
    a2s_ref[...] = back.reshape(n, 8, 128)
    a2r_ref[me] = a2s_ref[me]

    @pl.loop(1, n)
    def _(o):
        dd, dev = peer(o)
        pltpu.make_async_remote_copy(src_ref=a2s_ref.at[dd], dst_ref=a2r_ref.at[me], send_sem=a2_s, recv_sem=a2_r,
                                     device_id=dev, device_id_type=MESH).start()

    @pl.loop(0, T // CH)
    def _(c):
        tiles = []
        for g in range(CH):
            a = p_ref[pl.ds(64 + c * CH + g, 32, stride=64), :]
            b = p_ref[pl.ds(96 + c * CH + g, 32, stride=64), :]
            tiles.append(jnp.where(low32, a, swap(b)))
            tiles.append(jnp.where(low32, swap(a), b))
        k = lane_transform(jnp.concatenate(tiles, axis=0), kw_ref[1])
        y = jnp.concatenate([k[g * 64 : g * 64 + 64] for g in range(CH)], axis=1)
        y = mm(am_ref[1], rows3(y))
        for g in range(CH):
            s_ref[pl.ds(pl.multiple_of((c * CH + g) * 64, 64), 64), :] = y[:, g * 128 : g * 128 + 128]

    fm0t = nt(eye64, fm0)
    fm0pt = nt(qm, fm0)

    pltpu.make_async_copy(a2r_ref.at[pl.ds(0, n - 1)], a2r_ref.at[pl.ds(0, n - 1)], a2_r).wait()
    backs = jnp.sum(a2r_ref[...], axis=0)
    gamma = backs[6:7, :]
    corr = []
    for f in range(6):
        place = mapt[:, f : f + 1] == lanef
        corr.append(jnp.sum(jnp.where(place, backs[f : f + 1], 0.0), axis=1, keepdims=True))
    e01 = nn(fm0pt, jnp.where(low, corr[0], corr[1]) * fm11)
    e23 = nn(fm0t, jnp.where(low, corr[2], corr[3]) * fm11)
    e45 = nn(fm0t, jnp.where(low, corr[4], corr[5]) * fm11)
    eh, el = split(e45)
    eh = jnp.concatenate([eh, el], axis=0)

    @pl.loop(0, T // CH)
    def _(c):
        base = pl.multiple_of(c * (CH * 128), CH * 128)
        add = mm(eh, sel_ref[:, pl.ds(base, CH * 128)])
        for g in range(CH):
            at = pl.multiple_of((c * CH + g) * 64, 64)
            tile = add[:64, g * 128 : g * 128 + 128] + add[64:, g * 128 : g * 128 + 128]
            p_ref[pl.ds(at + 64, 64), :] = s_ref[pl.ds(at, 64), :] + tile

    p_ref[64:128, :] += jnp.where(low64, e23, 0.0)
    p_ref[T * 64 : T * 64 + 64, :] += jnp.where(low64, 0.0, e23)
    top, bottom = e01[:32], e01[32:]
    edge0 = p_ref[pl.ds(64, 32, stride=64), :] + jnp.where(low32, top, swap(bottom))
    edge1 = p_ref[pl.ds(64 + 63, 32, stride=64), :] + jnp.where(low32, swap(top), bottom)
    p_ref[pl.ds(64, 32, stride=64), :] = edge0
    p_ref[pl.ds(64 + 63, 32, stride=64), :] = edge1

    his_ref[0] = edge0
    his_ref[1] = edge1
    hjs_ref[0] = p_ref[64:128, :]
    hjs_ref[1] = p_ref[T * 64 : T * 64 + 64, :]

    sends = (
        (s > 0, s < nsub - 1, (s - 1, t), his_ref, hi_ref, 0, 1, 0),
        (s < nsub - 1, s > 0, (s + 1, t), his_ref, hi_ref, 1, 0, 1),
        (t > 0, t < ncg - 1, (s, t - 1), hjs_ref, hj_ref, 0, 1, 2),
        (t < ncg - 1, t > 0, (s, t + 1), hjs_ref, hj_ref, 1, 0, 3),
    )

    def halo(dev, src, dst, a, b, k):
        return pltpu.make_async_remote_copy(src_ref=src.at[a], dst_ref=dst.at[b], send_sem=h_s.at[k],
                                            recv_sem=h_r.at[k], device_id=dev, device_id_type=MESH)

    for does, gets, dev, src, dst, a, b, k in sends:
        @pl.when(does)
        def _():
            halo(dev, src, dst, a, b, k).start()

        @pl.when(jnp.logical_not(gets))
        def _():
            dst[b] = jnp.zeros(dst.shape[1:], f32)

    ccopy.wait()
    for does, gets, dev, src, dst, a, b, k in sends:
        @pl.when(gets)
        def _():
            halo(dev, src, dst, a, b, k).wait_recv()

    p_ref[0:64, :] = hj_ref[0]
    p_ref[(T + 1) * 64 : (T + 2) * 64, :] = hj_ref[1]

    row = iota((64, 128), 0)
    kpos = iota((64, 128), 1) & 63

    def stencil(q, acc):
        at = pl.multiple_of(q * 64, 64)
        x = p_ref[pl.ds(at + 64, 64), :]
        here = swap(x)
        before = swap(p_ref[pl.ds(at, 64), :])
        after = swap(p_ref[pl.ds(at + 128, 64), :])
        second = here + jnp.where(low64, before, after)
        up = jnp.where(row == 0, hi_ref[0, pl.ds(q, 1), :], pltpu.roll(x, 1, 0))
        down = jnp.where(row == 63, hi_ref[1, pl.ds(q, 1), :], pltpu.roll(x, 63, 0))
        third = jnp.where(kpos == 0, 0.0, pltpu.roll(x, 1, 1)) + jnp.where(kpos == 63, 0.0, pltpu.roll(x, 127, 1))
        cols_at = pl.ds(pl.multiple_of(q * 128, 128), 128)
        img = (cap_ref[:, cols_at] + 8.2) * x - (up + down) - 0.6 * second - 2.5 * third
        img_out[:, cols_at] = img
        p_out[:, cols_at] = x
        return acc + x * img

    cacc = lax.fori_loop(0, T, stencil, jnp.zeros((64, 128), f32))
    cpart = jnp.sum(cacc, axis=0, keepdims=True)
    cs_ref[...] = cpart
    cr_ref[me] = cpart

    @pl.loop(1, n)
    def _(o):
        _, dev = peer(o)
        pltpu.make_async_remote_copy(src_ref=cs_ref, dst_ref=cr_ref.at[me], send_sem=c_s, recv_sem=c_r,
                                     device_id=dev, device_id_type=MESH).start()

    pltpu.make_async_copy(cr_ref.at[pl.ds(0, n - 1)], cr_ref.at[pl.ds(0, n - 1)], c_r).wait()
    curv = jnp.sum(jnp.sum(cr_ref[...], axis=0), axis=1, keepdims=True)
    alpha_out[...] = jnp.broadcast_to(gamma / curv, (8, 128))

    pltpu.make_async_copy(ag_ref.at[pl.ds(0, n - 1)], ag_ref.at[pl.ds(0, n - 1)], ag_s).wait()
    pltpu.make_async_copy(a2r_ref.at[pl.ds(0, n - 1)], a2r_ref.at[pl.ds(0, n - 1)], a2_s).wait()
    pltpu.make_async_copy(cr_ref.at[pl.ds(0, n - 1)], cr_ref.at[pl.ds(0, n - 1)], c_s).wait()
    for does, gets, dev, src, dst, a, b, k in sends:
        @pl.when(does)
        def _():
            halo(dev, src, dst, a, b, k).wait_send()


def body(nsub, ncg, source, capacity, fd_weights, fd_modes, face_modes, coarse_map, fsai_cols, fsai_blocks):
    n = nsub * ncg
    nrow, nz = fsai_cols.shape
    vm = pl.BlockSpec(memory_space=pltpu.VMEM)
    hbm = pl.BlockSpec(memory_space=pl.ANY)
    field = jax.ShapeDtypeStruct(source.shape, f32)
    V = pltpu.VMEM
    dma = pltpu.SemaphoreType.DMA
    p, img, alpha = pl.pallas_call(
        functools.partial(kernel, nsub, ncg),
        out_shape=(field, field, jax.ShapeDtypeStruct((8, 128), f32)),
        in_specs=[vm] * 5 + [hbm] * 3,
        out_specs=(vm, vm, vm),
        scratch_shapes=[
            V((T * 64, 128), f32),
            V((T * 64, 128), f32),
            V((64, T * 128), f32),
            V(((T + 2) * 64, 128), f32),
            V((64, T * 128), f32),
            V(fsai_blocks.shape, f32),
            V((128, T * 128), bf16),
            V((4, 64, 192), bf16),
            V((2, 256, 256), bf16),
            V((n, 8, 128), f32),
            V((8, 128), f32),
            V((n, 8, 128), f32),
            V((n, 8, 128), f32),
            V((nrow, nz, 128), f32),
            V((128 // nz, nz, 128), f32),
            V((2, 32, 128), f32),
            V((2, 32, 128), f32),
            V((2, 64, 128), f32),
            V((2, 64, 128), f32),
            V((1, 128), f32),
            V((n, 1, 128), f32),
            dma((3,)),
            dma, dma, dma, dma,
            dma((4,)), dma((4,)),
            dma, dma,
        ],
        compiler_params=pltpu.CompilerParams(collective_id=0, has_side_effects=True,
                                             vmem_limit_bytes=48 * 1024 * 1024),
        cost_estimate=pl.CostEstimate(flops=10**9, bytes_accessed=8 * 2**20, transcendentals=0),
        name="step",
    )(source, fd_modes, face_modes, coarse_map, fsai_cols, capacity, fd_weights, fsai_blocks)
    a = alpha[0, 0]
    return a * p, source - a * img


def solution(mesh):
    in_specs = (
        P("sub", "cgrp"),
        P("sub", "cgrp"),
        P("sub", "cgrp"),
        P(),
        P(),
        P("sub", "cgrp", None, None),
        P(("sub", "cgrp"), None),
        P(("sub", "cgrp"), None, None, None),
    )
    out_specs = (P("sub", "cgrp"), P("sub", "cgrp"))
    step = functools.partial(body, mesh.shape["sub"], mesh.shape["cgrp"])
    return jax.shard_map(step, mesh=mesh, in_specs=in_specs, out_specs=out_specs, check_vma=False)
```

time: 439 us -> 42.1 us (0.10); the launches traced: 433 us -> 41.8 us
  waiting for transfers between devices: 213 us -> 0 us
  local copies, waits for them, and re-layouts: 95.1 us -> 7.46 us
  blocking collectives: 39.3 us -> 0 us
  matrix products: 33.6 us -> 0 us
  Pallas kernels: 0 us -> 31.4 us
  other arithmetic: 25.1 us -> 2.21 us
  between operations: 16 us -> 0.66 us
  starting transfers between devices: 11.1 us -> 0 us
    psum x2 -> x0, waiting for transfers between devices: 208 us -> none  [the longest x1 121 us: coarse_round(): lax.psum(coarse_apply(coarse, fsai_cols, fsai_blocks), ('sub', 'cgrp'))]
    psum x1 -> x0, blocking collectives: 39.3 us -> none  [inner_sum(): return lax.psum(jnp.sum(left * right), ('sub', 'cgrp'))]
    dot_general x10 -> x0, matrix products: 33.6 us -> none  [the longest x1 5.82 us: transform(): return jnp.einsum('ck,...abk->...abc', modes[2], blocks, precision=highest)]
    pallas_call x0 -> x1, Pallas kernels: none -> 31.4 us  [body(): pl.pallas_call(functools.partial(kernel, nsub, ncg), out_shape=(field, fi...]
    slice x11 -> x1, local copies, waits for them, and re-layouts: 17.1 us -> 0.59 us  [body(): a = alpha[0, 0]]
    reshape x5 -> x0, local copies, waits for them, and re-layouts: 14.4 us -> none  [the longest x2 6.28 us: body(): source = source.reshape(cube)]
    scatter-add x6 -> x0, local copies, waits for them, and re-layouts: 13.8 us -> none  [the longest x1 8.36 us: add_planes(): blocks = blocks.at[..., :, -1, :].add(planes[..., 3, :, :])]
    ppermute x4 -> x0, starting transfers between devices: 10.7 us -> none  [the longest x2 8.17 us: with_halo(): before = lax.ppermute(last, axis, up)]
  transfers between devices with their start and end apart: 6 -> 0, of which waited for: 4 -> 0; matrix products, arithmetic and copies ran while one was open for 11% -> 0% of each run, Pallas kernels for 0% -> 0%
where the time goes in v1:
time: 42.1 us; the launch traced here: 41.8 us
  Pallas kernels  31.4 us (75%)
  local copies, waits for them, and re-layouts  7.46 us (18%)
  other arithmetic  2.21 us (5%)
  between operations  0.66 us (2%)
    pallas_call x1, Pallas kernels, body(): pl.pallas_call(functools.partial(kernel, nsub, ncg), out_shape=(field, fi...  31.4 us
    unnamed x12, local copies, waits for them, and re-layouts  6.87 us
    sub x1, other arithmetic, body(): return (a * p, source - a * img)  2.21 us

profile of v1, /device:TPU:0, one launch (start us, length us, event | category | flops | bytes accessed | tf_op | source)
XLA Modules:
  0.0 41.8 jit_solution(17091337330355072208)
XLA Ops:
  0.6 0.7 %copy.11.map_ref = s32[1,1,6,128]{3,2,1,0:T(8,128)S(1)} copy(s32[1,1,6,128]{3,1,2,0:T(1,128)} %param.13) | data formatting | bytes 6144 | tf_op args[5]
  1.3 0.9 %copy.10.face_ref = f32[2,128,64]{2,1,0:T(8,128)S(1)} copy(f32[2,128,64]{1,2,0:T(8,128)} %param.12) | data formatting | bytes 131072 | tf_op args[4]
  2.3 0.0 copy-start
  2.3 1.2 %copy-done = f32[64,4096]{1,0:T(8,128)S(1)} copy-done((f32[64,4096]{1,0:T(8,128)S(1)}, f32[64,4096]{1,0:T(8,128)}, u32[]{:S(2)}) %copy-start) | copy-done | bytes 1048600
  3.5 0.0 copy-start.1
  3.5 1.2 %copy-done.1 = f32[64,4096]{1,0:T(8,128)S(1)} copy-done((f32[64,4096]{1,0:T(8,128)S(1)}, f32[64,4096]{1,0:T(8,128)}, u32[]{:S(2)}) %copy-start.1) | copy-done | bytes 1048600
  4.7 0.0 copy-start.2
  4.7 1.2 %copy-done.2 = f32[64,4096]{1,0:T(8,128)S(1)} copy-done((f32[64,4096]{1,0:T(8,128)S(1)}, f32[64,4096]{1,0:T(8,128)}, u32[]{:S(2)}) %copy-start.2) | copy-done | bytes 1048600
  5.9 0.0 copy-start.3
  5.9 0.9 %copy-done.3 = f32[3,64,64]{2,1,0:T(8,128)S(1)} copy-done((f32[3,64,64]{2,1,0:T(8,128)S(1)}, f32[3,64,64]{2,1,0:T(8,128)}, u32[]{:S(2)}) %copy-start.3) | copy-done | bytes 49176
  6.8 0.0 copy-start.4
  6.8 0.7 %copy-done.4 = s32[6,8]{1,0:T(8,128)S(1)} copy-done((s32[6,8]{1,0:T(8,128)S(1)}, s32[6,8]{1,0:T(8,128)}, u32[]{:S(2)}) %copy-start.4) | copy-done | bytes 216
  7.5 31.4 %step.1 = (f32[64,4096]{1,0:T(8,128)S(1)}, f32[64,4096]{1,0:T(8,128)S(1)}, f32[8,128]{1,0:T(8,128)S(1)}) custom-call(f32[64,4096]{1,0:T(8,128)S(1)} %copy-done, f32[3,64,64]{2,1,0:T(8,128)S(1)} %copy-done.3, f32[2,128,64]{2,1,0:T(8,128)S(1)} %copy.10.face_ref, s32[1,1,6,128]{3,2,1,0:T(8,128)S(1)} %copy.11.map_ref, s32[6,8]{1,0:T(8,128)S(1)} %copy-done.4, ...), custom_call_target="tpu_custom_call" | custom-call | flops 1000000000 | bytes 8388608 | tf_op jit(solution)/shard_map/step/pallas_call | solution.py:376
  38.9 0.6 %slice.3 = f32[1,1]{1,0:T(1,128)} slice(f32[8,128]{1,0:T(8,128)S(1)} %get-tuple-element.5), slice={[0:1], [0:1]} | slice | bytes 8 | tf_op jit(solution)/shard_map/slice | solution.py:413
  39.5 2.2 %multiply_subtract_fusion = (f32[64,4096]{1,0:T(8,128)}, f32[64,4096]{1,0:T(8,128)}) fusion(f32[64,4096]{1,0:T(8,128)S(1)} %copy-done, f32[64,4096]{1,0:T(8,128)S(1)} %get-tuple-element.7, f32[]{:T(128)} %bitcast, f32[64,4096]{1,0:T(8,128)S(1)} %get-tuple-element.6), kind=kLoop, calls=%fused_computation | loop fusion | flops 786432 | bytes 5242884 | tf_op jit(solution)/shard_map/sub | solution.py:414
Async XLA Ops:
  2.3 1.2 %copy-start = (f32[64,4096]{1,0:T(8,128)S(1)}, f32[64,4096]{1,0:T(8,128)}, u32[]{:S(2)}) copy-start(f32[64,4096]{1,0:T(8,128)} %x_ref.1) | copy-start | bytes 3145732
  3.5 1.2 %copy-start.1 = (f32[64,4096]{1,0:T(8,128)S(1)}, f32[64,4096]{1,0:T(8,128)}, u32[]{:S(2)}) copy-start(f32[64,4096]{1,0:T(8,128)} %cap_any.1) | copy-start | bytes 3145732
  4.7 1.2 %copy-start.2 = (f32[64,4096]{1,0:T(8,128)S(1)}, f32[64,4096]{1,0:T(8,128)}, u32[]{:S(2)}) copy-start(f32[64,4096]{1,0:T(8,128)} %wt_any.1) | copy-start | bytes 3145732
  5.9 0.9 %copy-start.3 = (f32[3,64,64]{2,1,0:T(8,128)S(1)}, f32[3,64,64]{2,1,0:T(8,128)}, u32[]{:S(2)}) copy-start(f32[3,64,64]{2,1,0:T(8,128)} %modes_ref.1) | copy-start | bytes 147460
  6.8 0.7 %copy-start.4 = (s32[6,8]{1,0:T(8,128)S(1)}, s32[6,8]{1,0:T(8,128)}, u32[]{:S(2)}) copy-start(s32[6,8]{1,0:T(8,128)} %cols_ref.1) | copy-start | bytes 580

commit v2 on v1

--- a/solution.py
+++ b/solution.py
@@ -63,12 +63,13 @@
     return r[:, :128] + r[:, 128:]
 
 
-def kernel(nsub, ncg, x_ref, modes_ref, face_ref, map_ref, cols_ref, cap_any, wt_any, blk_any,
+def kernel(nsub, ncg, x_any, modes_any, face_any, map_any, cols_any, cap_any, wt_any, blk_any,
            p_out, img_out, alpha_out,
+           x_ref, modes_ref, face_ref, map_ref, cols_ref,
            s_ref, z_ref, w_ref, p_ref, cap_ref, blk_ref, sel_ref, am_ref, kw_ref,
            ag_ref, send1_ref, a2s_ref, a2r_ref, pick_ref, spread_ref,
            hi_ref, his_ref, hj_ref, hjs_ref, cs_ref, cr_ref,
-           dsem, ag_s, ag_r, a2_s, a2_r, h_s, h_r, c_s, c_r):
+           dsem, ag_s, ag_r, a2_s, a2_r, h_s, h_r, c_s, c_r, osem):
     n = nsub * ncg
     s = lax.axis_index("sub")
     t = lax.axis_index("cgrp")
@@ -78,19 +79,20 @@
         d = lax.rem(me + o, n)
         return d, (lax.div(d, ncg), lax.rem(d, ncg))
 
+    early = []
+    for k, (src, dst) in enumerate(((face_any, face_ref), (map_any, map_ref), (x_any, x_ref),
+                                    (modes_any, modes_ref), (cols_any, cols_ref),
+                                    (wt_any, w_ref), (blk_any, blk_ref), (cap_any, cap_ref))):
+        early.append(pltpu.make_async_copy(src, dst, dsem.at[k]))
+        early[-1].start()
+    fcopy, mcopy, xcopy, ocopy, lcopy, wcopy, bcopy, ccopy = early
+
     barrier = pltpu.get_barrier_semaphore()
 
     @pl.loop(1, n)
     def _(o):
         _, dev = peer(o)
         pl.semaphore_signal(barrier, inc=1, device_id=dev, device_id_type=MESH)
-
-    wcopy = pltpu.make_async_copy(wt_any, w_ref, dsem.at[0])
-    bcopy = pltpu.make_async_copy(blk_any, blk_ref, dsem.at[1])
-    ccopy = pltpu.make_async_copy(cap_any, cap_ref, dsem.at[2])
-    wcopy.start()
-    bcopy.start()
-    ccopy.start()
 
     lane = iota((1, 128), 1)
     low = lane < 64
@@ -107,11 +109,10 @@
         hit = ((col >> 6) == (r & 63)) & ((col & 63) == 63 * (r >> 6))
         sel_ref[:, pl.ds(pl.multiple_of(c * 512, 512), 512)] = jnp.where(hit, 1.0, 0.0).astype(bf16)
 
-    for q in range(T):
-        s_ref[q * 64 : q * 64 + 64, :] = x_ref[:, q * 128 : q * 128 + 128]
-
-    fm0 = face_ref[0]
-    fm1 = face_ref[1]
+    fcopy.wait()
+    mcopy.wait()
+    fm0t = face_ref[0]
+    fm1t = face_ref[1]
     r64 = iota((64, 64), 0)
     c64 = iota((64, 64), 1)
     eye64 = jnp.where(r64 == c64, 1.0, 0.0)
@@ -119,24 +120,31 @@
     dup = jnp.where((iota((64, 128), 1) & 63) == iota((64, 128), 0), 1.0, 0.0)
     dupt = jnp.where((iota((128, 64), 0) & 63) == iota((128, 64), 1), 1.0, 0.0)
     eye128 = jnp.where(iota((128, 128), 0) == iota((128, 128), 1), 1.0, 0.0)
-    fm11 = nn(fm1, dup)
-    fm0p = nt(fm0, qm)
-
-    y0 = s_ref[pl.ds(0, 32, stride=64), :]
-    y1 = s_ref[pl.ds(63, 32, stride=64), :]
+    fm0pt = nn(qm, fm0t)
+    fm0 = nt(eye128, fm0t)
+    fm0p = nt(eye128, fm0pt)
+    fm11 = nt(eye128, jnp.concatenate([fm1t, fm1t], axis=0))
+
+    mapf = [(map_ref[f] & 127).astype(f32) for f in range(6)]
+    mapf = jnp.concatenate(mapf + [jnp.zeros((2, 128), f32)], axis=0)
+    mapt = nt(eye128, mapf)
+    lanef = iota((128, 128), 1).astype(f32)
+
+    xcopy.wait()
+    for q in range(T):
+        s_ref[q * 8 : q * 8 + 8, :] = x_ref[0:8, q * 128 : q * 128 + 128]
+        s_ref[256 + q * 8 : 256 + q * 8 + 8, :] = x_ref[56:64, q * 128 : q * 128 + 128]
+    y0 = s_ref[pl.ds(0, 32, stride=8), :]
+    y1 = s_ref[pl.ds(263, 32, stride=8), :]
     f01 = jnp.concatenate([jnp.where(low32, y0, swap(y1)), jnp.where(low32, swap(y0), y1)], axis=0)
-    f23 = jnp.where(low64, s_ref[0:64, :], s_ref[31 * 64 : 32 * 64, :])
+    f23 = jnp.where(low64, x_ref[:, :128], x_ref[:, 31 * 128 :])
     xh, xl = split(x_ref[...])
     f45 = mmt(jnp.concatenate([xh, xl], axis=0), sel_ref[...])
     f45 = f45[:64] + f45[64:]
 
-    mapf = (map_ref[0, 0] & 127).astype(f32)
-    mapf = jnp.concatenate([mapf, jnp.zeros((2, 128), f32)], axis=0)
-    mapt = nt(eye128, mapf)
-    lanef = iota((128, 128), 1).astype(f32)
     rows = []
     for pair, (left, plane) in enumerate(((fm0p, f01), (fm0, f23), (fm0, f45))):
-        u = nn(left, plane) * fm11
+        u = mm(left3(left), rows3(plane)) * fm11
         for half in range(2):
             keep = low if half == 0 else jnp.logical_not(low)
             val = jnp.sum(jnp.where(keep, u, 0.0), axis=1, keepdims=True)
@@ -155,6 +163,7 @@
         pltpu.make_async_remote_copy(src_ref=send1_ref, dst_ref=ag_ref.at[me], send_sem=ag_s, recv_sem=ag_r,
                                      device_id=dev, device_id_type=MESH).start()
 
+    ocopy.wait()
     m0, m1, m2 = modes_ref[0], modes_ref[1], modes_ref[2]
     am_ref[0] = left3(m0)
     am_ref[1] = left3(nt(eye64, m0))
@@ -195,6 +204,7 @@
 
     gacc = lax.fori_loop(0, T // CH, middle, jnp.zeros((64, 128), f32))
 
+    lcopy.wait()
     cols = cols_ref[...]
     nrow = cols.shape[0]
     nz = cols.shape[1]
@@ -255,9 +265,6 @@
         for g in range(CH):
             s_ref[pl.ds(pl.multiple_of((c * CH + g) * 64, 64), 64), :] = y[:, g * 128 : g * 128 + 128]
 
-    fm0t = nt(eye64, fm0)
-    fm0pt = nt(qm, fm0)
-
     pltpu.make_async_copy(a2r_ref.at[pl.ds(0, n - 1)], a2r_ref.at[pl.ds(0, n - 1)], a2_r).wait()
     backs = jnp.sum(a2r_ref[...], axis=0)
     gamma = backs[6:7, :]
@@ -265,9 +272,9 @@
     for f in range(6):
         place = mapt[:, f : f + 1] == lanef
         corr.append(jnp.sum(jnp.where(place, backs[f : f + 1], 0.0), axis=1, keepdims=True))
-    e01 = nn(fm0pt, jnp.where(low, corr[0], corr[1]) * fm11)
-    e23 = nn(fm0t, jnp.where(low, corr[2], corr[3]) * fm11)
-    e45 = nn(fm0t, jnp.where(low, corr[4], corr[5]) * fm11)
+    e01 = mm(left3(fm0pt), rows3(jnp.where(low, corr[0], corr[1]) * fm11))
+    e23 = mm(left3(fm0t), rows3(jnp.where(low, corr[2], corr[3]) * fm11))
+    e45 = mm(left3(fm0t), rows3(jnp.where(low, corr[4], corr[5]) * fm11))
     eh, el = split(e45)
     eh = jnp.concatenate([eh, el], axis=0)
 
@@ -337,8 +344,9 @@
         third = jnp.where(kpos == 0, 0.0, pltpu.roll(x, 1, 1)) + jnp.where(kpos == 63, 0.0, pltpu.roll(x, 127, 1))
         cols_at = pl.ds(pl.multiple_of(q * 128, 128), 128)
         img = (cap_ref[:, cols_at] + 8.2) * x - (up + down) - 0.6 * second - 2.5 * third
-        img_out[:, cols_at] = img
-        p_out[:, cols_at] = x
+        z_ref[pl.ds(at, 64), :] = img
+        pltpu.make_async_copy(p_ref.at[pl.ds(at + 64, 64), :], p_out.at[:, cols_at], osem.at[0]).start()
+        pltpu.make_async_copy(z_ref.at[pl.ds(at, 64), :], img_out.at[:, cols_at], osem.at[1]).start()
         return acc + x * img
 
     cacc = lax.fori_loop(0, T, stencil, jnp.zeros((64, 128), f32))
@@ -354,8 +362,10 @@
 
     pltpu.make_async_copy(cr_ref.at[pl.ds(0, n - 1)], cr_ref.at[pl.ds(0, n - 1)], c_r).wait()
     curv = jnp.sum(jnp.sum(cr_ref[...], axis=0), axis=1, keepdims=True)
-    alpha_out[...] = jnp.broadcast_to(gamma / curv, (8, 128))
-
+    alpha_out[...] = gamma[:, 0:1] / curv
+
+    pltpu.make_async_copy(z_ref, z_ref, osem.at[0]).wait()
+    pltpu.make_async_copy(z_ref, z_ref, osem.at[1]).wait()
     pltpu.make_async_copy(ag_ref.at[pl.ds(0, n - 1)], ag_ref.at[pl.ds(0, n - 1)], ag_s).wait()
     pltpu.make_async_copy(a2r_ref.at[pl.ds(0, n - 1)], a2r_ref.at[pl.ds(0, n - 1)], a2_s).wait()
     pltpu.make_async_copy(cr_ref.at[pl.ds(0, n - 1)], cr_ref.at[pl.ds(0, n - 1)], c_s).wait()
@@ -369,16 +379,21 @@
     n = nsub * ncg
     nrow, nz = fsai_cols.shape
     vm = pl.BlockSpec(memory_space=pltpu.VMEM)
-    hbm = pl.BlockSpec(memory_space=pl.ANY)
+    hbm = pl.BlockSpec(memory_space=pltpu.HBM)
     field = jax.ShapeDtypeStruct(source.shape, f32)
     V = pltpu.VMEM
     dma = pltpu.SemaphoreType.DMA
     p, img, alpha = pl.pallas_call(
         functools.partial(kernel, nsub, ncg),
-        out_shape=(field, field, jax.ShapeDtypeStruct((8, 128), f32)),
-        in_specs=[vm] * 5 + [hbm] * 3,
-        out_specs=(vm, vm, vm),
+        out_shape=(field, field, jax.ShapeDtypeStruct((1, 1), f32)),
+        in_specs=[hbm] * 8,
+        out_specs=(hbm, hbm, vm),
         scratch_shapes=[
+            V(source.shape, f32),
+            V(fd_modes.shape, f32),
+            V((2, 64, 128), f32),
+            V((6, 1, 128), jnp.int32),
+            V(fsai_cols.shape, jnp.int32),
             V((T * 64, 128), f32),
             V((T * 64, 128), f32),
             V((64, T * 128), f32),
@@ -400,16 +415,18 @@
             V((2, 64, 128), f32),
             V((1, 128), f32),
             V((n, 1, 128), f32),
-            dma((3,)),
+            dma((8,)),
             dma, dma, dma, dma,
             dma((4,)), dma((4,)),
             dma, dma,
+            dma((2,)),
         ],
         compiler_params=pltpu.CompilerParams(collective_id=0, has_side_effects=True,
-                                             vmem_limit_bytes=48 * 1024 * 1024),
+                                             vmem_limit_bytes=60 * 1024 * 1024),
         cost_estimate=pl.CostEstimate(flops=10**9, bytes_accessed=8 * 2**20, transcendentals=0),
         name="step",
-    )(source, fd_modes, face_modes, coarse_map, fsai_cols, capacity, fd_weights, fsai_blocks)
+    )(source, fd_modes, jnp.swapaxes(face_modes, 1, 2), coarse_map.reshape(-1, 1, coarse_map.shape[-1]),
+      fsai_cols, capacity, fd_weights, fsai_blocks)
     a = alpha[0, 0]
     return a * p, source - a * img
 

time: 42.1 us -> 36.6 us (0.87)
  local copies, waits for them, and re-layouts: 7.46 us -> 0.01 us
  other arithmetic: 2.21 us -> 3.63 us
  Pallas kernels: 31.4 us -> 32.2 us
    unnamed x12 -> x2, local copies, waits for them, and re-layouts: 6.87 us -> 0.01 us
    sub x1, other arithmetic: 2.21 us -> 3.63 us  [body(): return (a * p, source - a * img)]
    pallas_call x1, Pallas kernels: 31.4 us -> 32.2 us  [body(): pl.pallas_call(functools.partial(kernel, nsub, ncg), out_shape=(field, fi...]
    slice x1 -> x0, local copies, waits for them, and re-layouts: 0.59 us -> none  [body(): a = alpha[0, 0]]
where the time goes in v2:
time: 36.6 us; the launch traced here: 36.5 us
  Pallas kernels  32.2 us (88%)
  other arithmetic  3.63 us (10%)
  between operations  0.66 us (2%)
    pallas_call x1, Pallas kernels, body(): pl.pallas_call(functools.partial(kernel, nsub, ncg), out_shape=(field, fi...  32.2 us
    sub x1, other arithmetic, body(): return (a * p, source - a * img)  3.63 us

profile of v2, /device:TPU:0, one launch (start us, length us, event | category | flops | bytes accessed | tf_op | source)
XLA Modules:
  0.0 36.5 jit_solution(14206431359499013314)
XLA Ops:
  0.6 0.0 copy-start
  0.6 32.2 %step.1 = (f32[64,4096]{1,0:T(8,128)}, f32[64,4096]{1,0:T(8,128)}, f32[1,1]{1,0:T(1,128)}) custom-call(f32[64,4096]{1,0:T(8,128)} %x_any.1, f32[3,64,64]{2,1,0:T(8,128)} %modes_any.1, f32[2,64,128]{2,1,0:T(8,128)} %bitcast.3, s32[6,1,128]{2,1,0:T(1,128)} %bitcast.4, s32[6,8]{1,0:T(8,128)} %cols_any.1, f32[64,4096]{1,0:T(8,128)} %cap_any.1, ...), custom_call_target="tpu_custom_call" | custom-call | flops 1000000000 | bytes 8388608 | tf_op jit(solution)/shard_map/step/pallas_call | solution.py:386
  32.8 0.0 copy-done
  32.8 3.6 %multiply_subtract_fusion = (f32[64,4096]{1,0:T(8,128)}, f32[64,4096]{1,0:T(8,128)}) fusion(f32[64,4096]{1,0:T(8,128)S(1)} %copy-done, f32[64,4096]{1,0:T(8,128)} %get-tuple-element.7, f32[]{:T(128)} %bitcast.2, f32[64,4096]{1,0:T(8,128)} %get-tuple-element.6), kind=kLoop, calls=%fused_computation | loop fusion | flops 786432 | bytes 5242884 | tf_op jit(solution)/shard_map/sub | solution.py:431
Async XLA Ops:
  0.6 32.2 %copy-start = (f32[64,4096]{1,0:T(8,128)S(1)}, f32[64,4096]{1,0:T(8,128)}, u32[]{:S(2)}) copy-start(f32[64,4096]{1,0:T(8,128)} %x_any.1) | copy-start | bytes 3145732

commit v3 on v2

--- a/solution.py
+++ b/solution.py
@@ -69,7 +69,7 @@
            s_ref, z_ref, w_ref, p_ref, cap_ref, blk_ref, sel_ref, am_ref, kw_ref,
            ag_ref, send1_ref, a2s_ref, a2r_ref, pick_ref, spread_ref,
            hi_ref, his_ref, hj_ref, hjs_ref, cs_ref, cr_ref,
-           dsem, ag_s, ag_r, a2_s, a2_r, h_s, h_r, c_s, c_r, osem):
+           dsem, ag_s, ag_r, a2_s, a2_r, h_s, h_r, c_s, c_r):
     n = nsub * ncg
     s = lax.axis_index("sub")
     t = lax.axis_index("cgrp")
@@ -321,13 +321,8 @@
             dst[b] = jnp.zeros(dst.shape[1:], f32)
 
     ccopy.wait()
-    for does, gets, dev, src, dst, a, b, k in sends:
-        @pl.when(gets)
-        def _():
-            halo(dev, src, dst, a, b, k).wait_recv()
-
-    p_ref[0:64, :] = hj_ref[0]
-    p_ref[(T + 1) * 64 : (T + 2) * 64, :] = hj_ref[1]
+    p_ref[0:64, :] = jnp.zeros((64, 128), f32)
+    p_ref[(T + 1) * 64 : (T + 2) * 64, :] = jnp.zeros((64, 128), f32)
 
     row = iota((64, 128), 0)
     kpos = iota((64, 128), 1) & 63
@@ -339,18 +334,26 @@
         before = swap(p_ref[pl.ds(at, 64), :])
         after = swap(p_ref[pl.ds(at + 128, 64), :])
         second = here + jnp.where(low64, before, after)
-        up = jnp.where(row == 0, hi_ref[0, pl.ds(q, 1), :], pltpu.roll(x, 1, 0))
-        down = jnp.where(row == 63, hi_ref[1, pl.ds(q, 1), :], pltpu.roll(x, 63, 0))
+        up = jnp.where(row == 0, 0.0, pltpu.roll(x, 1, 0))
+        down = jnp.where(row == 63, 0.0, pltpu.roll(x, 63, 0))
         third = jnp.where(kpos == 0, 0.0, pltpu.roll(x, 1, 1)) + jnp.where(kpos == 63, 0.0, pltpu.roll(x, 127, 1))
         cols_at = pl.ds(pl.multiple_of(q * 128, 128), 128)
         img = (cap_ref[:, cols_at] + 8.2) * x - (up + down) - 0.6 * second - 2.5 * third
-        z_ref[pl.ds(at, 64), :] = img
-        pltpu.make_async_copy(p_ref.at[pl.ds(at + 64, 64), :], p_out.at[:, cols_at], osem.at[0]).start()
-        pltpu.make_async_copy(z_ref.at[pl.ds(at, 64), :], img_out.at[:, cols_at], osem.at[1]).start()
+        img_out[:, cols_at] = img
+        p_out[:, cols_at] = x
         return acc + x * img
 
-    cacc = lax.fori_loop(0, T, stencil, jnp.zeros((64, 128), f32))
-    cpart = jnp.sum(cacc, axis=0, keepdims=True)
+    cacc = lax.fori_loop(0, T, stencil, jnp.zeros((64, 128), f32), unroll=2)
+    for does, gets, dev, src, dst, a, b, k in sends:
+        @pl.when(gets)
+        def _():
+            halo(dev, src, dst, a, b, k).wait_recv()
+
+    fix0 = 0.6 * jnp.where(low64, swap(hj_ref[0]), 0.0)
+    fix1 = 0.6 * jnp.where(low64, 0.0, swap(hj_ref[1]))
+    cacc = cacc - hjs_ref[0] * fix0 - hjs_ref[1] * fix1
+    csum = his_ref[0] * hi_ref[0] + his_ref[1] * hi_ref[1]
+    cpart = jnp.sum(cacc, axis=0, keepdims=True) - jnp.sum(csum, axis=0, keepdims=True)
     cs_ref[...] = cpart
     cr_ref[me] = cpart
 
@@ -360,12 +363,17 @@
         pltpu.make_async_remote_copy(src_ref=cs_ref, dst_ref=cr_ref.at[me], send_sem=c_s, recv_sem=c_r,
                                      device_id=dev, device_id_type=MESH).start()
 
+    img_out[:, :128] = img_out[:, :128] - fix0
+    img_out[:, (T - 1) * 128 :] = img_out[:, (T - 1) * 128 :] - fix1
+    for q in range(T):
+        at = slice(q * 128, q * 128 + 128)
+        img_out[0:1, at] = img_out[0:1, at] - hi_ref[0, q : q + 1, :]
+        img_out[63:64, at] = img_out[63:64, at] - hi_ref[1, q : q + 1, :]
+
     pltpu.make_async_copy(cr_ref.at[pl.ds(0, n - 1)], cr_ref.at[pl.ds(0, n - 1)], c_r).wait()
     curv = jnp.sum(jnp.sum(cr_ref[...], axis=0), axis=1, keepdims=True)
     alpha_out[...] = gamma[:, 0:1] / curv
 
-    pltpu.make_async_copy(z_ref, z_ref, osem.at[0]).wait()
-    pltpu.make_async_copy(z_ref, z_ref, osem.at[1]).wait()
     pltpu.make_async_copy(ag_ref.at[pl.ds(0, n - 1)], ag_ref.at[pl.ds(0, n - 1)], ag_s).wait()
     pltpu.make_async_copy(a2r_ref.at[pl.ds(0, n - 1)], a2r_ref.at[pl.ds(0, n - 1)], a2_s).wait()
     pltpu.make_async_copy(cr_ref.at[pl.ds(0, n - 1)], cr_ref.at[pl.ds(0, n - 1)], c_s).wait()
@@ -387,7 +395,7 @@
         functools.partial(kernel, nsub, ncg),
         out_shape=(field, field, jax.ShapeDtypeStruct((1, 1), f32)),
         in_specs=[hbm] * 8,
-        out_specs=(hbm, hbm, vm),
+        out_specs=(vm, vm, vm),
         scratch_shapes=[
             V(source.shape, f32),
             V(fd_modes.shape, f32),
@@ -419,14 +427,14 @@
             dma, dma, dma, dma,
             dma((4,)), dma((4,)),
             dma, dma,
-            dma((2,)),
         ],
         compiler_params=pltpu.CompilerParams(collective_id=0, has_side_effects=True,
-                                             vmem_limit_bytes=60 * 1024 * 1024),
+                                             vmem_limit_bytes=48 * 1024 * 1024),
         cost_estimate=pl.CostEstimate(flops=10**9, bytes_accessed=8 * 2**20, transcendentals=0),
         name="step",
-    )(source, fd_modes, jnp.swapaxes(face_modes, 1, 2), coarse_map.reshape(-1, 1, coarse_map.shape[-1]),
-      fsai_cols, capacity, fd_weights, fsai_blocks)
+    )(*(pltpu.with_memory_space_constraint(v, pltpu.HBM) for v in (
+        source, fd_modes, jnp.swapaxes(face_modes, 1, 2), coarse_map.reshape(-1, 1, coarse_map.shape[-1]),
+        fsai_cols, capacity, fd_weights, fsai_blocks)))
     a = alpha[0, 0]
     return a * p, source - a * img
 

time: 36.6 us -> 31.7 us (0.87)
  Pallas kernels: 32.2 us -> 28.7 us
  other arithmetic: 3.63 us -> 2.17 us
    pallas_call x1, Pallas kernels: 32.2 us -> 28.7 us  [body(): pl.pallas_call(functools.partial(kernel, nsub, ncg), out_shape=(field, fi...]
    sub x1, other arithmetic: 3.63 us -> 2.17 us  [body(): return (a * p, source - a * img)]
where the time goes in v3:
time: 31.7 us; the launch traced here: 31.6 us
  Pallas kernels  28.7 us (91%)
  other arithmetic  2.17 us (7%)
  between operations  0.66 us (2%)
    pallas_call x1, Pallas kernels, body(): pl.pallas_call(functools.partial(kernel, nsub, ncg), out_shape=(field, fi...  28.7 us
    sub x1, other arithmetic, body(): return (a * p, source - a * img)  2.17 us

profile of v3, /device:TPU:0, one launch (start us, length us, event | category | flops | bytes accessed | tf_op | source)
XLA Modules:
  0.0 31.6 jit_solution(9118585756090247122)
XLA Ops:
  0.6 0.0 copy-start
  0.6 28.7 %step.1 = (f32[64,4096]{1,0:T(8,128)S(1)}, f32[64,4096]{1,0:T(8,128)S(1)}, f32[1,1]{1,0:T(1,128)}) custom-call(f32[64,4096]{1,0:T(8,128)} %x_any.1, f32[3,64,64]{2,1,0:T(8,128)} %modes_any.1, f32[2,64,128]{2,1,0:T(8,128)} %bitcast.3, s32[6,1,128]{2,1,0:T(1,128)} %bitcast.4, s32[6,8]{1,0:T(8,128)} %cols_any.1, f32[64,4096]{1,0:T(8,128)} %cap_any.1, ...), custom_call_target="tpu_custom_call" | custom-call | flops 1000000000 | bytes 8388608 | tf_op jit(solution)/shard_map/step/pallas_call | solution.py:394
  29.4 0.0 copy-done
  29.4 2.2 %multiply_subtract_fusion = (f32[64,4096]{1,0:T(8,128)}, f32[64,4096]{1,0:T(8,128)}) fusion(f32[64,4096]{1,0:T(8,128)S(1)} %copy-done, f32[64,4096]{1,0:T(8,128)S(1)} %get-tuple-element.7, f32[]{:T(128)} %bitcast.2, f32[64,4096]{1,0:T(8,128)S(1)} %get-tuple-element.6), kind=kLoop, calls=%fused_computation | loop fusion | flops 786432 | bytes 5242884 | tf_op jit(solution)/shard_map/sub | solution.py:439
Async XLA Ops:
  0.6 28.7 %copy-start = (f32[64,4096]{1,0:T(8,128)S(1)}, f32[64,4096]{1,0:T(8,128)}, u32[]{:S(2)}) copy-start(f32[64,4096]{1,0:T(8,128)} %x_any.1) | copy-start | bytes 3145732

commit v4 on v3

--- a/solution.py
+++ b/solution.py
@@ -86,6 +86,13 @@
         early.append(pltpu.make_async_copy(src, dst, dsem.at[k]))
         early[-1].start()
     fcopy, mcopy, xcopy, ocopy, lcopy, wcopy, bcopy, ccopy = early
+
+    def peers(step):
+        if n > 32:
+            pl.loop(1, n)(step)
+        else:
+            for o in range(1, n):
+                step(o)
 
     barrier = pltpu.get_barrier_semaphore()
 
@@ -121,13 +128,13 @@
     dupt = jnp.where((iota((128, 64), 0) & 63) == iota((128, 64), 1), 1.0, 0.0)
     eye128 = jnp.where(iota((128, 128), 0) == iota((128, 128), 1), 1.0, 0.0)
     fm0pt = nn(qm, fm0t)
-    fm0 = nt(eye128, fm0t)
-    fm0p = nt(eye128, fm0pt)
-    fm11 = nt(eye128, jnp.concatenate([fm1t, fm1t], axis=0))
+    fm0 = fm0t.T
+    fm0p = fm0pt.T
+    fm11 = jnp.concatenate([fm1t, fm1t], axis=0).T
 
     mapf = [(map_ref[f] & 127).astype(f32) for f in range(6)]
     mapf = jnp.concatenate(mapf + [jnp.zeros((2, 128), f32)], axis=0)
-    mapt = nt(eye128, mapf)
+    mapt = mmt(eye128.astype(bf16), mapf.astype(bf16))
     lanef = iota((128, 128), 1).astype(f32)
 
     xcopy.wait()
@@ -157,7 +164,7 @@
 
     pl.semaphore_wait(barrier, n - 1)
 
-    @pl.loop(1, n)
+    @peers
     def _(o):
         _, dev = peer(o)
         pltpu.make_async_remote_copy(src_ref=send1_ref, dst_ref=ag_ref.at[me], send_sem=ag_s, recv_sem=ag_r,
@@ -222,8 +229,13 @@
     g1 = jnp.where(colv == own, 1.0, 0.0)
     g1 = jnp.concatenate([g1, jnp.zeros((128 - kk, n * 8), f32)], axis=0)
 
+    g2 = g1.T.astype(bf16)
+    g2 = jnp.concatenate([g2, g2], axis=1)
+    g1 = g1.astype(bf16)
+
     pltpu.make_async_copy(ag_ref.at[pl.ds(0, n - 1)], ag_ref.at[pl.ds(0, n - 1)], ag_r).wait()
-    picked = nn(g1, ag_ref[...].reshape(n * 8, 128))
+    th, tl = split(ag_ref[...].reshape(n * 8, 128))
+    picked = mm(g1, th) + mm(g1, tl)
     pick_ref[...] = picked[:kk].reshape(nrow, nz, 128)
     bcopy.wait()
     spread_ref[...] = jnp.zeros_like(spread_ref)
@@ -240,12 +252,12 @@
 
     iacc = lax.fori_loop(0, nrow, coarse_row, jnp.zeros((128, 1), f32))
     gpart = jnp.sum(iacc, keepdims=True) + jnp.sum(gacc, keepdims=True)
-    back = nn(g1.T, spread_ref[...].reshape(128, 128))
+    back = mm(g2, jnp.concatenate(split(spread_ref[...].reshape(128, 128)), axis=0))
     back = jnp.where((iota((n * 8, 128), 0) & 7) == 6, gpart, back)
     a2s_ref[...] = back.reshape(n, 8, 128)
     a2r_ref[me] = a2s_ref[me]
 
-    @pl.loop(1, n)
+    @peers
     def _(o):
         dd, dev = peer(o)
         pltpu.make_async_remote_copy(src_ref=a2s_ref.at[dd], dst_ref=a2r_ref.at[me], send_sem=a2_s, recv_sem=a2_r,
@@ -357,7 +369,7 @@
     cs_ref[...] = cpart
     cr_ref[me] = cpart
 
-    @pl.loop(1, n)
+    @peers
     def _(o):
         _, dev = peer(o)
         pltpu.make_async_remote_copy(src_ref=cs_ref, dst_ref=cr_ref.at[me], send_sem=c_s, recv_sem=c_r,

time: 31.7 us -> 31.5 us (level)
  no operation moved by 1% of the time
where the time goes in v4:
time: 31.5 us; the launch traced here: 31.3 us
  Pallas kernels  28.5 us (90%)
  other arithmetic  2.17 us (7%)
  between operations  0.66 us (2%)
    pallas_call x1, Pallas kernels, body(): pl.pallas_call(functools.partial(kernel, nsub, ncg), out_shape=(field, fi...  28.5 us
    sub x1, other arithmetic, body(): return (a * p, source - a * img)  2.17 us

profile of v4, /device:TPU:0, one launch (start us, length us, event | category | flops | bytes accessed | tf_op | source)
XLA Modules:
  0.0 31.3 jit_solution(14061800741282024004)
XLA Ops:
  0.6 0.0 copy-start
  0.6 28.5 %step.1 = (f32[64,4096]{1,0:T(8,128)S(1)}, f32[64,4096]{1,0:T(8,128)S(1)}, f32[1,1]{1,0:T(1,128)}) custom-call(f32[64,4096]{1,0:T(8,128)} %x_any.1, f32[3,64,64]{2,1,0:T(8,128)} %modes_any.1, f32[2,64,128]{2,1,0:T(8,128)} %bitcast.3, s32[6,1,128]{2,1,0:T(1,128)} %bitcast.4, s32[6,8]{1,0:T(8,128)} %cols_any.1, f32[64,4096]{1,0:T(8,128)} %cap_any.1, ...), custom_call_target="tpu_custom_call" | custom-call | flops 1000000000 | bytes 8388608 | tf_op jit(solution)/shard_map/step/pallas_call | solution.py:406
  29.1 0.0 copy-done
  29.1 2.2 %multiply_subtract_fusion = (f32[64,4096]{1,0:T(8,128)}, f32[64,4096]{1,0:T(8,128)}) fusion(f32[64,4096]{1,0:T(8,128)S(1)} %copy-done, f32[64,4096]{1,0:T(8,128)S(1)} %get-tuple-element.7, f32[]{:T(128)} %bitcast.2, f32[64,4096]{1,0:T(8,128)S(1)} %get-tuple-element.6), kind=kLoop, calls=%fused_computation | loop fusion | flops 786432 | bytes 5242884 | tf_op jit(solution)/shard_map/sub | solution.py:451
Async XLA Ops:
  0.6 28.5 %copy-start = (f32[64,4096]{1,0:T(8,128)S(1)}, f32[64,4096]{1,0:T(8,128)}, u32[]{:S(2)}) copy-start(f32[64,4096]{1,0:T(8,128)} %x_any.1) | copy-start | bytes 3145732

commit v5 on v4

--- a/solution.py
+++ b/solution.py
@@ -209,7 +209,7 @@
             p_ref[pl.ds(pl.multiple_of(64 + (c * CH + g) * 64, 64), 64), :] = y[:, g * 128 : g * 128 + 128]
         return acc
 
-    gacc = lax.fori_loop(0, T // CH, middle, jnp.zeros((64, 128), f32))
+    gacc = lax.fori_loop(0, T // CH // 2, middle, jnp.zeros((64, 128), f32))
 
     lcopy.wait()
     cols = cols_ref[...]
@@ -251,9 +251,7 @@
         return acc + img * img
 
     iacc = lax.fori_loop(0, nrow, coarse_row, jnp.zeros((128, 1), f32))
-    gpart = jnp.sum(iacc, keepdims=True) + jnp.sum(gacc, keepdims=True)
     back = mm(g2, jnp.concatenate(split(spread_ref[...].reshape(128, 128)), axis=0))
-    back = jnp.where((iota((n * 8, 128), 0) & 7) == 6, gpart, back)
     a2s_ref[...] = back.reshape(n, 8, 128)
     a2r_ref[me] = a2s_ref[me]
 
@@ -262,6 +260,9 @@
         dd, dev = peer(o)
         pltpu.make_async_remote_copy(src_ref=a2s_ref.at[dd], dst_ref=a2r_ref.at[me], send_sem=a2_s, recv_sem=a2_r,
                                      device_id=dev, device_id_type=MESH).start()
+
+    gacc = lax.fori_loop(T // CH // 2, T // CH, middle, gacc)
+    gpart = jnp.sum(iacc, keepdims=True) + jnp.sum(gacc, keepdims=True)
 
     @pl.loop(0, T // CH)
     def _(c):
@@ -279,7 +280,6 @@
 
     pltpu.make_async_copy(a2r_ref.at[pl.ds(0, n - 1)], a2r_ref.at[pl.ds(0, n - 1)], a2_r).wait()
     backs = jnp.sum(a2r_ref[...], axis=0)
-    gamma = backs[6:7, :]
     corr = []
     for f in range(6):
         place = mapt[:, f : f + 1] == lanef
@@ -366,6 +366,7 @@
     cacc = cacc - hjs_ref[0] * fix0 - hjs_ref[1] * fix1
     csum = his_ref[0] * hi_ref[0] + his_ref[1] * hi_ref[1]
     cpart = jnp.sum(cacc, axis=0, keepdims=True) - jnp.sum(csum, axis=0, keepdims=True)
+    cpart = jnp.where(low, cpart + swap(cpart), gpart * (1.0 / 64.0))
     cs_ref[...] = cpart
     cr_ref[me] = cpart
 
@@ -383,8 +384,10 @@
         img_out[63:64, at] = img_out[63:64, at] - hi_ref[1, q : q + 1, :]
 
     pltpu.make_async_copy(cr_ref.at[pl.ds(0, n - 1)], cr_ref.at[pl.ds(0, n - 1)], c_r).wait()
-    curv = jnp.sum(jnp.sum(cr_ref[...], axis=0), axis=1, keepdims=True)
-    alpha_out[...] = gamma[:, 0:1] / curv
+    both = jnp.sum(cr_ref[...], axis=0)
+    curv = jnp.sum(jnp.where(low, both, 0.0), axis=1, keepdims=True)
+    gamma = jnp.sum(jnp.where(low, 0.0, both), axis=1, keepdims=True)
+    alpha_out[...] = gamma / curv
 
     pltpu.make_async_copy(ag_ref.at[pl.ds(0, n - 1)], ag_ref.at[pl.ds(0, n - 1)], ag_s).wait()
     pltpu.make_async_copy(a2r_ref.at[pl.ds(0, n - 1)], a2r_ref.at[pl.ds(0, n - 1)], a2_s).wait()

time: 31.5 us -> 30.7 us (0.975)
  Pallas kernels: 28.5 us -> 27.8 us
    pallas_call x1, Pallas kernels: 28.5 us -> 27.8 us  [body(): pl.pallas_call(functools.partial(kernel, nsub, ncg), out_shape=(field, fi...]
where the time goes in v5:
time: 30.7 us; the launch traced here: 30.6 us
  Pallas kernels  27.8 us (91%)
  other arithmetic  2.17 us (7%)
  between operations  0.66 us (2%)
    pallas_call x1, Pallas kernels, body(): pl.pallas_call(functools.partial(kernel, nsub, ncg), out_shape=(field, fi...  27.8 us
    sub x1, other arithmetic, body(): return (a * p, source - a * img)  2.17 us

profile of v5, /device:TPU:0, one launch (start us, length us, event | category | flops | bytes accessed | tf_op | source)
XLA Modules:
  0.0 30.6 jit_solution(10050003567044812864)
XLA Ops:
  0.6 0.0 copy-start
  0.6 27.8 %step.1 = (f32[64,4096]{1,0:T(8,128)S(1)}, f32[64,4096]{1,0:T(8,128)S(1)}, f32[1,1]{1,0:T(1,128)}) custom-call(f32[64,4096]{1,0:T(8,128)} %x_any.1, f32[3,64,64]{2,1,0:T(8,128)} %modes_any.1, f32[2,64,128]{2,1,0:T(8,128)} %bitcast.3, s32[6,1,128]{2,1,0:T(1,128)} %bitcast.4, s32[6,8]{1,0:T(8,128)} %cols_any.1, f32[64,4096]{1,0:T(8,128)} %cap_any.1, ...), custom_call_target="tpu_custom_call" | custom-call | flops 1000000000 | bytes 8388608 | tf_op jit(solution)/shard_map/step/pallas_call | solution.py:409
  28.4 0.0 copy-done
  28.4 2.2 %multiply_subtract_fusion = (f32[64,4096]{1,0:T(8,128)}, f32[64,4096]{1,0:T(8,128)}) fusion(f32[64,4096]{1,0:T(8,128)S(1)} %copy-done, f32[64,4096]{1,0:T(8,128)S(1)} %get-tuple-element.7, f32[]{:T(128)} %bitcast.2, f32[64,4096]{1,0:T(8,128)S(1)} %get-tuple-element.6), kind=kLoop, calls=%fused_computation | loop fusion | flops 786432 | bytes 5242884 | tf_op jit(solution)/shard_map/sub | solution.py:454
Async XLA Ops:
  0.6 27.8 %copy-start = (f32[64,4096]{1,0:T(8,128)S(1)}, f32[64,4096]{1,0:T(8,128)}, u32[]{:S(2)}) copy-start(f32[64,4096]{1,0:T(8,128)} %x_any.1) | copy-start | bytes 3145732
